TPU v7x, 32 devices: a whole 2x2x4 slice. The times are simulated.
32 devices in a mesh: flow: 16 (over z, y, x), lat: 2 (over core).
Axes of the slice: x: 2, y: 2, z: 4, core: 2. Of those that a mesh axis runs over, the one named last changes fastest.
Arguments:
- concentration: float32 [3, 256, 64, 128], P(None, 'flow', 'lat'), may hold values from 0 to 2
- courant: float32 [3, 256, 64, 128], P(None, 'flow', 'lat'), may hold values from 500 to 4000
- rates: float32 [2, 256, 64, 128], P(None, 'flow', 'lat'), may hold values from 0.2 to 3
- spread: float32 [64, 128], P('lat'), may hold values from 0.02 to 0.2
- inlet: float32 [3, 64, 128], P(None, 'lat'), may hold values from 200 to 2000
Outputs:
- fresh: float32 [3, 256, 64, 128], P(None, 'flow', 'lat')
All inputs are finite; a program needn't handle non-finite values.
Results may differ from a plain program's by a relative error of at most 0.000066.
Values sent between devices are 32-bit elements; how exact they have to be, the bound alone decides.
A program may use at most 64 MiB of HBM per device.

v0:
```python
import jax
import jax.numpy as jnp
from jax import lax
from jax.sharding import PartitionSpec as P


def padded_2(block, sides, width):
    for axis, dim in sides:
        count = lax.axis_size(axis)
        forward = [(i, i + 1) for i in range(count - 1)]
        backward = [(target, source) for source, target in forward]
        low = lax.ppermute(
            lax.slice_in_dim(block, block.shape[dim] - width, None, axis=dim), axis, forward
        )
        high = lax.ppermute(lax.slice_in_dim(block, 0, width, axis=dim), axis, backward)
        block = jnp.concatenate([low, block, high], axis=dim)
    return block


def from_behind(block, axis, distance):
    devices = range(lax.axis_size(axis))
    route = [(i - distance, i) for i in devices if i - distance in devices]
    return lax.ppermute(block, axis, route)


def cell_values(flux, src, coeffs):
    cour_a, cour_p, cour_v, rate_ap, rate_pv = coeffs
    first = (src[0] + flux[0]) / (1.0 + cour_a + rate_ap)
    second = (src[1] + flux[1] + rate_ap * first) / (1.0 + cour_p + rate_pv)
    third = (src[2] + flux[2] + rate_pv * second) / (1.0 + cour_v)
    return (first, second, third)


def cell_flux(flux, src, coeffs):
    first, second, third = cell_values(flux, src, coeffs)
    return (coeffs[0] * first, coeffs[1] * second, coeffs[2] * third)


def apply_map(matrix, offset, flux):
    out_a = matrix[0] * flux[0] + offset[0]
    out_p = matrix[1] * flux[0] + matrix[2] * flux[1] + offset[1]
    out_v = matrix[3] * flux[0] + matrix[4] * flux[1] + matrix[5] * flux[2] + offset[2]
    return jnp.stack([out_a, out_p, out_v])


def per_device(concentration, courant, rates, spread, inlet):
    padded = padded_2(concentration, (("lat", 2),), 1)
    zpadded = jnp.pad(concentration, ((0, 0), (0, 0), (0, 0), (1, 1)))
    beside = padded[:, :, 2:, :] + padded[:, :, :-2, :] + zpadded[..., 2:] + zpadded[..., :-2]
    source = concentration + spread[None, None] * (beside - 4.0 * concentration)
    cells = concentration.shape[1]
    ones = jnp.ones_like(spread)
    zeros = jnp.zeros_like(spread)
    nothing = (0.0, 0.0, 0.0)

    def coeffs_at(index):
        return (
            courant[0, index],
            courant[1, index],
            courant[2, index],
            rates[0, index],
            rates[1, index],
        )

    col_a = (ones, zeros, zeros)
    col_p = (zeros, ones, zeros)
    col_v = (zeros, zeros, ones)
    shifted = (zeros, zeros, zeros)
    for index in range(cells):
        coeffs = coeffs_at(index)
        col_a = cell_flux(col_a, nothing, coeffs)
        col_p = cell_flux(col_p, nothing, coeffs)
        col_v = cell_flux(col_v, nothing, coeffs)
        shifted = cell_flux(shifted, source[:, index], coeffs)
    matrix = jnp.stack([col_a[0], col_a[1], col_p[1], col_a[2], col_p[2], col_v[2]])
    offset = jnp.stack(shifted)
    position = lax.axis_index("flow")
    start = jnp.where(position == 0, inlet, jnp.zeros_like(inlet))

    def relay_step(turn, incoming):
        outgoing = apply_map(matrix, offset, incoming)
        arrived = from_behind(outgoing, "flow", 1)
        return jnp.where(position == 0, inlet, arrived)

    incoming = lax.fori_loop(0, lax.axis_size("flow") - 1, relay_step, start)
    flux = (incoming[0], incoming[1], incoming[2])
    values = []
    for index in range(cells):
        coeffs = coeffs_at(index)
        first, second, third = cell_values(flux, source[:, index], coeffs)
        values.append(jnp.stack([first, second, third]))
        flux = (coeffs[0] * first, coeffs[1] * second, coeffs[2] * third)
    return jnp.stack(values, axis=1)


def solution(mesh):
    in_specs = (
        P(None, "flow", "lat", None),
        P(None, "flow", "lat", None),
        P(None, "flow", "lat", None),
        P("lat", None),
        P(None, "lat", None),
    )
    out_specs = P(None, "flow", "lat", None)
    return jax.shard_map(
        per_device, mesh=mesh, in_specs=in_specs, out_specs=out_specs, check_vma=False
    )
```

profile of v0, /device:TPU:8, one launch (start us, length us, event | category | flops | bytes accessed | tf_op | source)
XLA Modules:
  0.0 131.3 jit_solution(7994766622120647635)
XLA Ops:
  0.0 1.1 fusion.562
  1.1 1.3 collective-permute-start.1
  2.4 3.0 %collective-permute-start.2 = (f32[3,16,1,128]{3,2,1,0:T(1,128)S(1)}, f32[3,16,1,128]{3,2,1,0:T(1,128)S(1)}, u32[]{:S(2)}, u32[]{:S(2)}) collective-permute-start(f32[3,16,1,128]{3,2,1,0:T(1,128)S(1)} %get-tuple-element.349), channel_id=1, source_target_pairs={{0,1},{2,3},{4,5},{6,7},{8,9},{10,11},{12,13},{14,15},{16,17},{18,... | collective-permute-start | bytes 73736 | tf_op jit(solution)/shard_map/ppermute | solution.py:12
  5.5 0.8 collective-permute-done.2
  6.2 2.9 %fusion.7 = f32[3,16,32,128]{3,2,1,0:T(8,128)S(1)} fusion(f32[3,16,32,128]{3,2,1,0:T(8,128)} %param.7, f32[3,16,1,128]{3,2,1,0:T(1,128)S(1)} %collective-permute-done.2, f32[3,16,1,128]{3,2,1,0:T(1,128)S(1)} %collective-permute-done.1, f32[32,128]{1,0:T(8,128)} %param.10), kind=kLoop, calls=%fused_computation.20 | loop fusion | flops 1769472 | bytes 1638400 | tf_op jit(solution)/shard_map/add | solution.py:50
  9.2 0.1 fusion.406
  9.4 0.2 fusion.289
  9.5 0.1 fusion.155
  9.7 0.2 fusion.260
  9.9 0.1 fusion.383
  10.0 0.1 fusion.379
  10.1 0.1 fusion.254
  10.2 0.1 fusion.257
  10.4 0.6 copy-done.2
  11.0 118.3 %while.12 = (s32[]{:T(128)}, f32[3,32,128]{2,1,0:T(8,128)S(1)}, pred[]{:T(512)}, f32[32,128]{1,0:T(8,128)S(1)}, f32[32,128]{1,0:T(8,128)S(1)}, /*index=5*/f32[32...) while((s32[]{:T(128)}, f32[3,32,128]{2,1,0:T(8,128)S(1)}, ...), condition=%wide.region_1.2_spmd, body=%wide.region_0.1_spmd.sunk | while | flops 86018 | bytes 688302 | solution.py:85
  11.0 3.4 %collective-permute-start = (f32[3,32,128]{2,1,0:T(8,128)S(1)}, f32[3,32,128]{2,1,0:T(8,128)S(1)}, u32[]{:S(2)}, u32[]{:S(2)}) collective-permute-start(f32[3,32,128]{2,1,0:T(8,128)S(1)} %pad_maximum_fusion.4), channel_id=1, source_target_pairs={{0,2},{2,4},{4,6},{6,8},{8,10},{10,12},{12,14},{14,16},{16,18},{18... | collective-permute-start | bytes 147464 | tf_op jit(solution)/shard_map/while/body/eval_jaxpr/ppermute | solution.py:23
  14.4 4.4 %collective-permute-done = f32[3,32,128]{2,1,0:T(8,128)S(1)} collective-permute-done((f32[3,32,128]{2,1,0:T(8,128)S(1)}, f32[3,32,128]{2,1,0:T(8,128)S(1)}, u32[]{:S(2)}, u32[]{:S(2)}) %collective-permute-start) | collective-permute-done | bytes 49184 | tf_op jit(solution)/shard_map/while/body/eval_jaxpr/ppermute | solution.py:23
  18.9 1.9 %collective-permute-start = (f32[3,32,128]{2,1,0:T(8,128)S(1)}, f32[3,32,128]{2,1,0:T(8,128)S(1)}, u32[]{:S(2)}, u32[]{:S(2)}) collective-permute-start(f32[3,32,128]{2,1,0:T(8,128)S(1)} %pad_maximum_fusion.4), channel_id=1, source_target_pairs={{0,2},{2,4},{4,6},{6,8},{8,10},{10,12},{12,14},{14,16},{16,18},{18... | collective-permute-start | bytes 147464 | tf_op jit(solution)/shard_map/while/body/eval_jaxpr/ppermute | solution.py:23
  20.8 5.9 %collective-permute-done = f32[3,32,128]{2,1,0:T(8,128)S(1)} collective-permute-done((f32[3,32,128]{2,1,0:T(8,128)S(1)}, f32[3,32,128]{2,1,0:T(8,128)S(1)}, u32[]{:S(2)}, u32[]{:S(2)}) %collective-permute-start) | collective-permute-done | bytes 49184 | tf_op jit(solution)/shard_map/while/body/eval_jaxpr/ppermute | solution.py:23
  26.7 1.9 %collective-permute-start = (f32[3,32,128]{2,1,0:T(8,128)S(1)}, f32[3,32,128]{2,1,0:T(8,128)S(1)}, u32[]{:S(2)}, u32[]{:S(2)}) collective-permute-start(f32[3,32,128]{2,1,0:T(8,128)S(1)} %pad_maximum_fusion.4), channel_id=1, source_target_pairs={{0,2},{2,4},{4,6},{6,8},{8,10},{10,12},{12,14},{14,16},{16,18},{18... | collective-permute-start | bytes 147464 | tf_op jit(solution)/shard_map/while/body/eval_jaxpr/ppermute | solution.py:23
  28.7 5.9 %collective-permute-done = f32[3,32,128]{2,1,0:T(8,128)S(1)} collective-permute-done((f32[3,32,128]{2,1,0:T(8,128)S(1)}, f32[3,32,128]{2,1,0:T(8,128)S(1)}, u32[]{:S(2)}, u32[]{:S(2)}) %collective-permute-start) | collective-permute-done | bytes 49184 | tf_op jit(solution)/shard_map/while/body/eval_jaxpr/ppermute | solution.py:23
  34.6 1.9 %collective-permute-start = (f32[3,32,128]{2,1,0:T(8,128)S(1)}, f32[3,32,128]{2,1,0:T(8,128)S(1)}, u32[]{:S(2)}, u32[]{:S(2)}) collective-permute-start(f32[3,32,128]{2,1,0:T(8,128)S(1)} %pad_maximum_fusion.4), channel_id=1, source_target_pairs={{0,2},{2,4},{4,6},{6,8},{8,10},{10,12},{12,14},{14,16},{16,18},{18... | collective-permute-start | bytes 147464 | tf_op jit(solution)/shard_map/while/body/eval_jaxpr/ppermute | solution.py:23
  36.5 5.9 %collective-permute-done = f32[3,32,128]{2,1,0:T(8,128)S(1)} collective-permute-done((f32[3,32,128]{2,1,0:T(8,128)S(1)}, f32[3,32,128]{2,1,0:T(8,128)S(1)}, u32[]{:S(2)}, u32[]{:S(2)}) %collective-permute-start) | collective-permute-done | bytes 49184 | tf_op jit(solution)/shard_map/while/body/eval_jaxpr/ppermute | solution.py:23
  42.4 1.9 %collective-permute-start = (f32[3,32,128]{2,1,0:T(8,128)S(1)}, f32[3,32,128]{2,1,0:T(8,128)S(1)}, u32[]{:S(2)}, u32[]{:S(2)}) collective-permute-start(f32[3,32,128]{2,1,0:T(8,128)S(1)} %pad_maximum_fusion.4), channel_id=1, source_target_pairs={{0,2},{2,4},{4,6},{6,8},{8,10},{10,12},{12,14},{14,16},{16,18},{18... | collective-permute-start | bytes 147464 | tf_op jit(solution)/shard_map/while/body/eval_jaxpr/ppermute | solution.py:23
  44.4 5.9 %collective-permute-done = f32[3,32,128]{2,1,0:T(8,128)S(1)} collective-permute-done((f32[3,32,128]{2,1,0:T(8,128)S(1)}, f32[3,32,128]{2,1,0:T(8,128)S(1)}, u32[]{:S(2)}, u32[]{:S(2)}) %collective-permute-start) | collective-permute-done | bytes 49184 | tf_op jit(solution)/shard_map/while/body/eval_jaxpr/ppermute | solution.py:23
  50.3 1.9 %collective-permute-start = (f32[3,32,128]{2,1,0:T(8,128)S(1)}, f32[3,32,128]{2,1,0:T(8,128)S(1)}, u32[]{:S(2)}, u32[]{:S(2)}) collective-permute-start(f32[3,32,128]{2,1,0:T(8,128)S(1)} %pad_maximum_fusion.4), channel_id=1, source_target_pairs={{0,2},{2,4},{4,6},{6,8},{8,10},{10,12},{12,14},{14,16},{16,18},{18... | collective-permute-start | bytes 147464 | tf_op jit(solution)/shard_map/while/body/eval_jaxpr/ppermute | solution.py:23
  52.2 6.1 %collective-permute-done = f32[3,32,128]{2,1,0:T(8,128)S(1)} collective-permute-done((f32[3,32,128]{2,1,0:T(8,128)S(1)}, f32[3,32,128]{2,1,0:T(8,128)S(1)}, u32[]{:S(2)}, u32[]{:S(2)}) %collective-permute-start) | collective-permute-done | bytes 49184 | tf_op jit(solution)/shard_map/while/body/eval_jaxpr/ppermute | solution.py:23
  58.3 1.9 %collective-permute-start = (f32[3,32,128]{2,1,0:T(8,128)S(1)}, f32[3,32,128]{2,1,0:T(8,128)S(1)}, u32[]{:S(2)}, u32[]{:S(2)}) collective-permute-start(f32[3,32,128]{2,1,0:T(8,128)S(1)} %pad_maximum_fusion.4), channel_id=1, source_target_pairs={{0,2},{2,4},{4,6},{6,8},{8,10},{10,12},{12,14},{14,16},{16,18},{18... | collective-permute-start | bytes 147464 | tf_op jit(solution)/shard_map/while/body/eval_jaxpr/ppermute | solution.py:23
  60.2 5.9 %collective-permute-done = f32[3,32,128]{2,1,0:T(8,128)S(1)} collective-permute-done((f32[3,32,128]{2,1,0:T(8,128)S(1)}, f32[3,32,128]{2,1,0:T(8,128)S(1)}, u32[]{:S(2)}, u32[]{:S(2)}) %collective-permute-start) | collective-permute-done | bytes 49184 | tf_op jit(solution)/shard_map/while/body/eval_jaxpr/ppermute | solution.py:23
  66.2 1.9 %collective-permute-start = (f32[3,32,128]{2,1,0:T(8,128)S(1)}, f32[3,32,128]{2,1,0:T(8,128)S(1)}, u32[]{:S(2)}, u32[]{:S(2)}) collective-permute-start(f32[3,32,128]{2,1,0:T(8,128)S(1)} %pad_maximum_fusion.4), channel_id=1, source_target_pairs={{0,2},{2,4},{4,6},{6,8},{8,10},{10,12},{12,14},{14,16},{16,18},{18... | collective-permute-start | bytes 147464 | tf_op jit(solution)/shard_map/while/body/eval_jaxpr/ppermute | solution.py:23
  68.1 5.9 %collective-permute-done = f32[3,32,128]{2,1,0:T(8,128)S(1)} collective-permute-done((f32[3,32,128]{2,1,0:T(8,128)S(1)}, f32[3,32,128]{2,1,0:T(8,128)S(1)}, u32[]{:S(2)}, u32[]{:S(2)}) %collective-permute-start) | collective-permute-done | bytes 49184 | tf_op jit(solution)/shard_map/while/body/eval_jaxpr/ppermute | solution.py:23
  74.0 1.9 %collective-permute-start = (f32[3,32,128]{2,1,0:T(8,128)S(1)}, f32[3,32,128]{2,1,0:T(8,128)S(1)}, u32[]{:S(2)}, u32[]{:S(2)}) collective-permute-start(f32[3,32,128]{2,1,0:T(8,128)S(1)} %pad_maximum_fusion.4), channel_id=1, source_target_pairs={{0,2},{2,4},{4,6},{6,8},{8,10},{10,12},{12,14},{14,16},{16,18},{18... | collective-permute-start | bytes 147464 | tf_op jit(solution)/shard_map/while/body/eval_jaxpr/ppermute | solution.py:23
  75.9 5.9 %collective-permute-done = f32[3,32,128]{2,1,0:T(8,128)S(1)} collective-permute-done((f32[3,32,128]{2,1,0:T(8,128)S(1)}, f32[3,32,128]{2,1,0:T(8,128)S(1)}, u32[]{:S(2)}, u32[]{:S(2)}) %collective-permute-start) | collective-permute-done | bytes 49184 | tf_op jit(solution)/shard_map/while/body/eval_jaxpr/ppermute | solution.py:23
  81.9 1.9 %collective-permute-start = (f32[3,32,128]{2,1,0:T(8,128)S(1)}, f32[3,32,128]{2,1,0:T(8,128)S(1)}, u32[]{:S(2)}, u32[]{:S(2)}) collective-permute-start(f32[3,32,128]{2,1,0:T(8,128)S(1)} %pad_maximum_fusion.4), channel_id=1, source_target_pairs={{0,2},{2,4},{4,6},{6,8},{8,10},{10,12},{12,14},{14,16},{16,18},{18... | collective-permute-start | bytes 147464 | tf_op jit(solution)/shard_map/while/body/eval_jaxpr/ppermute | solution.py:23
  83.8 5.9 %collective-permute-done = f32[3,32,128]{2,1,0:T(8,128)S(1)} collective-permute-done((f32[3,32,128]{2,1,0:T(8,128)S(1)}, f32[3,32,128]{2,1,0:T(8,128)S(1)}, u32[]{:S(2)}, u32[]{:S(2)}) %collective-permute-start) | collective-permute-done | bytes 49184 | tf_op jit(solution)/shard_map/while/body/eval_jaxpr/ppermute | solution.py:23
  89.7 1.9 %collective-permute-start = (f32[3,32,128]{2,1,0:T(8,128)S(1)}, f32[3,32,128]{2,1,0:T(8,128)S(1)}, u32[]{:S(2)}, u32[]{:S(2)}) collective-permute-start(f32[3,32,128]{2,1,0:T(8,128)S(1)} %pad_maximum_fusion.4), channel_id=1, source_target_pairs={{0,2},{2,4},{4,6},{6,8},{8,10},{10,12},{12,14},{14,16},{16,18},{18... | collective-permute-start | bytes 147464 | tf_op jit(solution)/shard_map/while/body/eval_jaxpr/ppermute | solution.py:23
  91.6 5.9 %collective-permute-done = f32[3,32,128]{2,1,0:T(8,128)S(1)} collective-permute-done((f32[3,32,128]{2,1,0:T(8,128)S(1)}, f32[3,32,128]{2,1,0:T(8,128)S(1)}, u32[]{:S(2)}, u32[]{:S(2)}) %collective-permute-start) | collective-permute-done | bytes 49184 | tf_op jit(solution)/shard_map/while/body/eval_jaxpr/ppermute | solution.py:23
  97.6 1.9 %collective-permute-start = (f32[3,32,128]{2,1,0:T(8,128)S(1)}, f32[3,32,128]{2,1,0:T(8,128)S(1)}, u32[]{:S(2)}, u32[]{:S(2)}) collective-permute-start(f32[3,32,128]{2,1,0:T(8,128)S(1)} %pad_maximum_fusion.4), channel_id=1, source_target_pairs={{0,2},{2,4},{4,6},{6,8},{8,10},{10,12},{12,14},{14,16},{16,18},{18... | collective-permute-start | bytes 147464 | tf_op jit(solution)/shard_map/while/body/eval_jaxpr/ppermute | solution.py:23
  99.5 6.2 %collective-permute-done = f32[3,32,128]{2,1,0:T(8,128)S(1)} collective-permute-done((f32[3,32,128]{2,1,0:T(8,128)S(1)}, f32[3,32,128]{2,1,0:T(8,128)S(1)}, u32[]{:S(2)}, u32[]{:S(2)}) %collective-permute-start) | collective-permute-done | bytes 49184 | tf_op jit(solution)/shard_map/while/body/eval_jaxpr/ppermute | solution.py:23
  105.8 1.9 %collective-permute-start = (f32[3,32,128]{2,1,0:T(8,128)S(1)}, f32[3,32,128]{2,1,0:T(8,128)S(1)}, u32[]{:S(2)}, u32[]{:S(2)}) collective-permute-start(f32[3,32,128]{2,1,0:T(8,128)S(1)} %pad_maximum_fusion.4), channel_id=1, source_target_pairs={{0,2},{2,4},{4,6},{6,8},{8,10},{10,12},{12,14},{14,16},{16,18},{18... | collective-permute-start | bytes 147464 | tf_op jit(solution)/shard_map/while/body/eval_jaxpr/ppermute | solution.py:23
  107.7 5.9 %collective-permute-done = f32[3,32,128]{2,1,0:T(8,128)S(1)} collective-permute-done((f32[3,32,128]{2,1,0:T(8,128)S(1)}, f32[3,32,128]{2,1,0:T(8,128)S(1)}, u32[]{:S(2)}, u32[]{:S(2)}) %collective-permute-start) | collective-permute-done | bytes 49184 | tf_op jit(solution)/shard_map/while/body/eval_jaxpr/ppermute | solution.py:23
  113.7 1.9 %collective-permute-start = (f32[3,32,128]{2,1,0:T(8,128)S(1)}, f32[3,32,128]{2,1,0:T(8,128)S(1)}, u32[]{:S(2)}, u32[]{:S(2)}) collective-permute-start(f32[3,32,128]{2,1,0:T(8,128)S(1)} %pad_maximum_fusion.4), channel_id=1, source_target_pairs={{0,2},{2,4},{4,6},{6,8},{8,10},{10,12},{12,14},{14,16},{16,18},{18... | collective-permute-start | bytes 147464 | tf_op jit(solution)/shard_map/while/body/eval_jaxpr/ppermute | solution.py:23
  115.6 5.9 %collective-permute-done = f32[3,32,128]{2,1,0:T(8,128)S(1)} collective-permute-done((f32[3,32,128]{2,1,0:T(8,128)S(1)}, f32[3,32,128]{2,1,0:T(8,128)S(1)}, u32[]{:S(2)}, u32[]{:S(2)}) %collective-permute-start) | collective-permute-done | bytes 49184 | tf_op jit(solution)/shard_map/while/body/eval_jaxpr/ppermute | solution.py:23
  121.5 1.9 %collective-permute-start = (f32[3,32,128]{2,1,0:T(8,128)S(1)}, f32[3,32,128]{2,1,0:T(8,128)S(1)}, u32[]{:S(2)}, u32[]{:S(2)}) collective-permute-start(f32[3,32,128]{2,1,0:T(8,128)S(1)} %pad_maximum_fusion.4), channel_id=1, source_target_pairs={{0,2},{2,4},{4,6},{6,8},{8,10},{10,12},{12,14},{14,16},{16,18},{18... | collective-permute-start | bytes 147464 | tf_op jit(solution)/shard_map/while/body/eval_jaxpr/ppermute | solution.py:23
  123.4 5.9 %collective-permute-done = f32[3,32,128]{2,1,0:T(8,128)S(1)} collective-permute-done((f32[3,32,128]{2,1,0:T(8,128)S(1)}, f32[3,32,128]{2,1,0:T(8,128)S(1)}, u32[]{:S(2)}, u32[]{:S(2)}) %collective-permute-start) | collective-permute-done | bytes 49184 | tf_op jit(solution)/shard_map/while/body/eval_jaxpr/ppermute | solution.py:23
  129.4 0.2 bitcast_divide_fusion
  129.9 0.9 copy-done.3
  130.7 0.6 fusion.24
  (72 shorter events, 0.8 us)
Async XLA Ops:
  1.1 4.4 %collective-permute-start.1 = (f32[3,16,1,128]{3,2,1,0:T(1,128)S(1)}, f32[3,16,1,128]{3,2,1,0:T(1,128)S(1)}, u32[]{:S(2)}, u32[]{:S(2)}) collective-permute-start(f32[3,16,1,128]{3,2,1,0:T(1,128)S(1)} %get-tuple-element.348), channel_id=1, source_target_pairs={{1,0},{3,2},{5,4},{7,6},{9,8},{11,10},{13,12},{15,14},{17,16},{19,... | collective-permute-start | bytes 73736 | tf_op jit(solution)/shard_map/ppermute | solution.py:15
  2.4 3.9 %collective-permute-start.2 = (f32[3,16,1,128]{3,2,1,0:T(1,128)S(1)}, f32[3,16,1,128]{3,2,1,0:T(1,128)S(1)}, u32[]{:S(2)}, u32[]{:S(2)}) collective-permute-start(f32[3,16,1,128]{3,2,1,0:T(1,128)S(1)} %get-tuple-element.349), channel_id=1, source_target_pairs={{0,1},{2,3},{4,5},{6,7},{8,9},{10,11},{12,13},{14,15},{16,17},{18,... | collective-permute-start | bytes 73736 | tf_op jit(solution)/shard_map/ppermute | solution.py:12
  5.4 3.8 %copy-start = (f32[2,16,32,128]{3,2,1,0:T(8,128)S(1)}, f32[2,16,32,128]{3,2,1,0:T(8,128)}, u32[]{:S(2)}) copy-start(f32[2,16,32,128]{3,2,1,0:T(8,128)} %param.9) | copy-start | bytes 1572868
  5.4 3.8 %copy-start.1 = (f32[3,16,32,128]{3,2,1,0:T(8,128)S(1)}, f32[3,16,32,128]{3,2,1,0:T(8,128)}, u32[]{:S(2)}) copy-start(f32[3,16,32,128]{3,2,1,0:T(8,128)} %param.8) | copy-start | bytes 2359300
  10.2 0.8 copy-start.2
  11.0 7.8 %collective-permute-start = (f32[3,32,128]{2,1,0:T(8,128)S(1)}, f32[3,32,128]{2,1,0:T(8,128)S(1)}, u32[]{:S(2)}, u32[]{:S(2)}) collective-permute-start(f32[3,32,128]{2,1,0:T(8,128)S(1)} %pad_maximum_fusion.4), channel_id=1, source_target_pairs={{0,2},{2,4},{4,6},{6,8},{8,10},{10,12},{12,14},{14,16},{16,18},{18... | collective-permute-start | bytes 147464 | tf_op jit(solution)/shard_map/while/body/eval_jaxpr/ppermute | solution.py:23
  18.9 7.8 %collective-permute-start = (f32[3,32,128]{2,1,0:T(8,128)S(1)}, f32[3,32,128]{2,1,0:T(8,128)S(1)}, u32[]{:S(2)}, u32[]{:S(2)}) collective-permute-start(f32[3,32,128]{2,1,0:T(8,128)S(1)} %pad_maximum_fusion.4), channel_id=1, source_target_pairs={{0,2},{2,4},{4,6},{6,8},{8,10},{10,12},{12,14},{14,16},{16,18},{18... | collective-permute-start | bytes 147464 | tf_op jit(solution)/shard_map/while/body/eval_jaxpr/ppermute | solution.py:23
  26.7 7.8 %collective-permute-start = (f32[3,32,128]{2,1,0:T(8,128)S(1)}, f32[3,32,128]{2,1,0:T(8,128)S(1)}, u32[]{:S(2)}, u32[]{:S(2)}) collective-permute-start(f32[3,32,128]{2,1,0:T(8,128)S(1)} %pad_maximum_fusion.4), channel_id=1, source_target_pairs={{0,2},{2,4},{4,6},{6,8},{8,10},{10,12},{12,14},{14,16},{16,18},{18... | collective-permute-start | bytes 147464 | tf_op jit(solution)/shard_map/while/body/eval_jaxpr/ppermute | solution.py:23
  34.6 7.8 %collective-permute-start = (f32[3,32,128]{2,1,0:T(8,128)S(1)}, f32[3,32,128]{2,1,0:T(8,128)S(1)}, u32[]{:S(2)}, u32[]{:S(2)}) collective-permute-start(f32[3,32,128]{2,1,0:T(8,128)S(1)} %pad_maximum_fusion.4), channel_id=1, source_target_pairs={{0,2},{2,4},{4,6},{6,8},{8,10},{10,12},{12,14},{14,16},{16,18},{18... | collective-permute-start | bytes 147464 | tf_op jit(solution)/shard_map/while/body/eval_jaxpr/ppermute | solution.py:23
  42.4 7.8 %collective-permute-start = (f32[3,32,128]{2,1,0:T(8,128)S(1)}, f32[3,32,128]{2,1,0:T(8,128)S(1)}, u32[]{:S(2)}, u32[]{:S(2)}) collective-permute-start(f32[3,32,128]{2,1,0:T(8,128)S(1)} %pad_maximum_fusion.4), channel_id=1, source_target_pairs={{0,2},{2,4},{4,6},{6,8},{8,10},{10,12},{12,14},{14,16},{16,18},{18... | collective-permute-start | bytes 147464 | tf_op jit(solution)/shard_map/while/body/eval_jaxpr/ppermute | solution.py:23
  50.3 8.0 %collective-permute-start = (f32[3,32,128]{2,1,0:T(8,128)S(1)}, f32[3,32,128]{2,1,0:T(8,128)S(1)}, u32[]{:S(2)}, u32[]{:S(2)}) collective-permute-start(f32[3,32,128]{2,1,0:T(8,128)S(1)} %pad_maximum_fusion.4), channel_id=1, source_target_pairs={{0,2},{2,4},{4,6},{6,8},{8,10},{10,12},{12,14},{14,16},{16,18},{18... | collective-permute-start | bytes 147464 | tf_op jit(solution)/shard_map/while/body/eval_jaxpr/ppermute | solution.py:23
  58.3 7.8 %collective-permute-start = (f32[3,32,128]{2,1,0:T(8,128)S(1)}, f32[3,32,128]{2,1,0:T(8,128)S(1)}, u32[]{:S(2)}, u32[]{:S(2)}) collective-permute-start(f32[3,32,128]{2,1,0:T(8,128)S(1)} %pad_maximum_fusion.4), channel_id=1, source_target_pairs={{0,2},{2,4},{4,6},{6,8},{8,10},{10,12},{12,14},{14,16},{16,18},{18... | collective-permute-start | bytes 147464 | tf_op jit(solution)/shard_map/while/body/eval_jaxpr/ppermute | solution.py:23
  66.2 7.8 %collective-permute-start = (f32[3,32,128]{2,1,0:T(8,128)S(1)}, f32[3,32,128]{2,1,0:T(8,128)S(1)}, u32[]{:S(2)}, u32[]{:S(2)}) collective-permute-start(f32[3,32,128]{2,1,0:T(8,128)S(1)} %pad_maximum_fusion.4), channel_id=1, source_target_pairs={{0,2},{2,4},{4,6},{6,8},{8,10},{10,12},{12,14},{14,16},{16,18},{18... | collective-permute-start | bytes 147464 | tf_op jit(solution)/shard_map/while/body/eval_jaxpr/ppermute | solution.py:23
  74.0 7.8 %collective-permute-start = (f32[3,32,128]{2,1,0:T(8,128)S(1)}, f32[3,32,128]{2,1,0:T(8,128)S(1)}, u32[]{:S(2)}, u32[]{:S(2)}) collective-permute-start(f32[3,32,128]{2,1,0:T(8,128)S(1)} %pad_maximum_fusion.4), channel_id=1, source_target_pairs={{0,2},{2,4},{4,6},{6,8},{8,10},{10,12},{12,14},{14,16},{16,18},{18... | collective-permute-start | bytes 147464 | tf_op jit(solution)/shard_map/while/body/eval_jaxpr/ppermute | solution.py:23
  81.9 7.8 %collective-permute-start = (f32[3,32,128]{2,1,0:T(8,128)S(1)}, f32[3,32,128]{2,1,0:T(8,128)S(1)}, u32[]{:S(2)}, u32[]{:S(2)}) collective-permute-start(f32[3,32,128]{2,1,0:T(8,128)S(1)} %pad_maximum_fusion.4), channel_id=1, source_target_pairs={{0,2},{2,4},{4,6},{6,8},{8,10},{10,12},{12,14},{14,16},{16,18},{18... | collective-permute-start | bytes 147464 | tf_op jit(solution)/shard_map/while/body/eval_jaxpr/ppermute | solution.py:23
  89.7 7.8 %collective-permute-start = (f32[3,32,128]{2,1,0:T(8,128)S(1)}, f32[3,32,128]{2,1,0:T(8,128)S(1)}, u32[]{:S(2)}, u32[]{:S(2)}) collective-permute-start(f32[3,32,128]{2,1,0:T(8,128)S(1)} %pad_maximum_fusion.4), channel_id=1, source_target_pairs={{0,2},{2,4},{4,6},{6,8},{8,10},{10,12},{12,14},{14,16},{16,18},{18... | collective-permute-start | bytes 147464 | tf_op jit(solution)/shard_map/while/body/eval_jaxpr/ppermute | solution.py:23
  97.6 8.2 %collective-permute-start = (f32[3,32,128]{2,1,0:T(8,128)S(1)}, f32[3,32,128]{2,1,0:T(8,128)S(1)}, u32[]{:S(2)}, u32[]{:S(2)}) collective-permute-start(f32[3,32,128]{2,1,0:T(8,128)S(1)} %pad_maximum_fusion.4), channel_id=1, source_target_pairs={{0,2},{2,4},{4,6},{6,8},{8,10},{10,12},{12,14},{14,16},{16,18},{18... | collective-permute-start | bytes 147464 | tf_op jit(solution)/shard_map/while/body/eval_jaxpr/ppermute | solution.py:23
  105.8 7.8 %collective-permute-start = (f32[3,32,128]{2,1,0:T(8,128)S(1)}, f32[3,32,128]{2,1,0:T(8,128)S(1)}, u32[]{:S(2)}, u32[]{:S(2)}) collective-permute-start(f32[3,32,128]{2,1,0:T(8,128)S(1)} %pad_maximum_fusion.4), channel_id=1, source_target_pairs={{0,2},{2,4},{4,6},{6,8},{8,10},{10,12},{12,14},{14,16},{16,18},{18... | collective-permute-start | bytes 147464 | tf_op jit(solution)/shard_map/while/body/eval_jaxpr/ppermute | solution.py:23
  113.7 7.8 %collective-permute-start = (f32[3,32,128]{2,1,0:T(8,128)S(1)}, f32[3,32,128]{2,1,0:T(8,128)S(1)}, u32[]{:S(2)}, u32[]{:S(2)}) collective-permute-start(f32[3,32,128]{2,1,0:T(8,128)S(1)} %pad_maximum_fusion.4), channel_id=1, source_target_pairs={{0,2},{2,4},{4,6},{6,8},{8,10},{10,12},{12,14},{14,16},{16,18},{18... | collective-permute-start | bytes 147464 | tf_op jit(solution)/shard_map/while/body/eval_jaxpr/ppermute | solution.py:23
  121.5 7.8 %collective-permute-start = (f32[3,32,128]{2,1,0:T(8,128)S(1)}, f32[3,32,128]{2,1,0:T(8,128)S(1)}, u32[]{:S(2)}, u32[]{:S(2)}) collective-permute-start(f32[3,32,128]{2,1,0:T(8,128)S(1)} %pad_maximum_fusion.4), channel_id=1, source_target_pairs={{0,2},{2,4},{4,6},{6,8},{8,10},{10,12},{12,14},{14,16},{16,18},{18... | collective-permute-start | bytes 147464 | tf_op jit(solution)/shard_map/while/body/eval_jaxpr/ppermute | solution.py:23
  129.8 0.9 copy-start.3
where the time goes:
time: 132 us; the launch traced here: 131 us
  waiting for transfers between devices  87.7 us (66%)
  starting transfers between devices  34.6 us (26%)
  other arithmetic  5.61 us (4%)
  local copies, waits for them, and re-layouts  2.59 us (2%)
    ppermute x15, waiting for transfers between devices, from_behind(): return lax.ppermute(block, axis, route)  86.9 us
    ppermute x15, starting transfers between devices, from_behind(): return lax.ppermute(block, axis, route)  30.3 us
    ppermute x1, starting transfers between devices, padded_2(): lax.ppermute(lax.slice_in_dim(block, block.shape[dim] - width, None, axis...  3.03 us
    add x1, other arithmetic, per_device(): source = concentration + spread[None, None] * (beside - 4.0 * concentration)  2.94 us
  transfers between devices with their start and end apart: 17, of which 16 were waited for; matrix products, arithmetic and copies ran while one was open for 0% of the time, Pallas kernels for 0%

commit v1 on v0

v1 whole, which is shorter than its diff:
```python
import functools
import jax
import jax.numpy as jnp
from jax import lax
from jax.experimental import pallas as pl
from jax.experimental.pallas import tpu as pltpu
from jax.sharding import PartitionSpec as P

MESH = pl.DeviceIdType.MESH
GROUP = 4
EDGE = 8


def apply_map(m, q):
    return (
        m[0] * q[0] + m[6],
        m[1] * q[0] + m[2] * q[1] + m[7],
        m[3] * q[0] + m[4] * q[1] + m[5] * q[2] + m[8],
    )


def after(m, n):
    lower = (
        m[0] * n[0],
        m[1] * n[0] + m[2] * n[1],
        m[2] * n[2],
        m[3] * n[0] + m[4] * n[1] + m[5] * n[3],
        m[4] * n[2] + m[5] * n[4],
        m[5] * n[5],
    )
    return lower + apply_map(m, n[6:])


def kernel(
    groups, group, lats,
    conc, courant, rates, spread, inlet, out,
    pad, cour, rate, spr, inl, local, mine, maps, total, totals, fluxes, entering,
    load_sem, halo_send, halo_recv, a_send, a_recv, b_send, b_recv, c_send, c_recv,
):
    cells, rows, width = cour.shape[1:]
    part = rows // group
    flow = lax.axis_index("flow")
    lat = lax.axis_index("lat")
    inner = lax.rem(flow, group)
    outer = lax.div(flow, group)

    loads = [
        pltpu.make_async_copy(src, dst, load_sem.at[i])
        for i, (src, dst) in enumerate((
            (courant, cour), (rates, rate), (conc, pad.at[:, :, EDGE:EDGE + rows]),
            (spread, spr), (inlet, inl),
        ))
    ]
    for load in loads:
        load.start()

    barrier = pltpu.get_barrier_semaphore()
    for step in range(1, group):
        peer = outer * group + lax.rem(inner + step, group)
        pl.semaphore_signal(barrier, inc=1, device_id={"flow": peer}, device_id_type=MESH)
    for step in range(1, groups):
        peer = lax.rem(outer + step, groups) * group + inner
        pl.semaphore_signal(barrier, inc=1, device_id={"flow": peer}, device_id_type=MESH)

    @pl.when(lat > 0)
    def _():
        pl.semaphore_signal(barrier, inc=1, device_id={"lat": lat - 1}, device_id_type=MESH)

    @pl.when(lat < lats - 1)
    def _():
        pl.semaphore_signal(barrier, inc=1, device_id={"lat": lat + 1}, device_id_type=MESH)

    beside = jnp.where(lat > 0, 1, 0) + jnp.where(lat < lats - 1, 1, 0)
    pl.semaphore_wait(barrier, group - 1 + groups - 1 + beside)

    to_high = pltpu.make_async_remote_copy(
        src_ref=conc.at[:, :, rows - EDGE:rows], dst_ref=pad.at[:, :, 0:EDGE],
        send_sem=halo_send.at[0], recv_sem=halo_recv.at[0],
        device_id={"lat": lat + 1}, device_id_type=MESH,
    )
    to_low = pltpu.make_async_remote_copy(
        src_ref=conc.at[:, :, 0:EDGE], dst_ref=pad.at[:, :, EDGE + rows:2 * EDGE + rows],
        send_sem=halo_send.at[1], recv_sem=halo_recv.at[1],
        device_id={"lat": lat - 1}, device_id_type=MESH,
    )
    nothing = jnp.zeros((3, cells, EDGE, width), jnp.float32)

    @pl.when(lat < lats - 1)
    def _():
        to_high.start()

    @pl.when(lat > 0)
    def _():
        to_low.start()

    @pl.when(lat == 0)
    def _():
        pad[:, :, 0:EDGE] = nothing

    @pl.when(lat == lats - 1)
    def _():
        pad[:, :, EDGE + rows:2 * EDGE + rows] = nothing

    for load in loads:
        load.wait()

    @pl.when(lat > 0)
    def _():
        to_high.wait_recv()

    @pl.when(lat < lats - 1)
    def _():
        to_low.wait_recv()

    scale = spr[...]
    lane = lax.broadcasted_iota(jnp.int32, (rows, width), 1)
    first, last = lane == 0, lane == width - 1

    def source(k, i):
        mid = pad[k, i, EDGE:EDGE + rows]
        left = jnp.where(first, 0.0, pltpu.roll(mid, 1, 1))
        right = jnp.where(last, 0.0, pltpu.roll(mid, width - 1, 1))
        near = pad[k, i, EDGE - 1:EDGE - 1 + rows] + pad[k, i, EDGE + 1:EDGE + 1 + rows]
        return mid + scale * (near + left + right - 4.0 * mid)

    def cell(i, state):
        m00, m10, m11, m20, m21, m22, w0, w1, w2 = state
        c0, c1, c2 = cour[0, i], cour[1, i], cour[2, i]
        k0, k1 = rate[0, i], rate[1, i]
        r0, r1, r2 = 1.0 / (1.0 + c0 + k0), 1.0 / (1.0 + c1 + k1), 1.0 / (1.0 + c2)
        u00 = m00 * r0
        u10 = (m10 + k0 * u00) * r1
        u20 = (m20 + k1 * u10) * r2
        u11 = m11 * r1
        u21 = (m21 + k1 * u11) * r2
        u22 = m22 * r2
        v0 = (source(0, i) + w0) * r0
        v1 = (source(1, i) + w1 + k0 * v0) * r1
        v2 = (source(2, i) + w2 + k1 * v1) * r2
        values = (u00, u10, u11, u20, u21, u22, v0, v1, v2)
        for q, value in enumerate(values):
            local[q, i] = value
        factors = (c0, c1, c1, c2, c2, c2, c0, c1, c2)
        return tuple(f * v for f, v in zip(factors, values))

    one = jnp.ones((rows, width), jnp.float32)
    zero = jnp.zeros((rows, width), jnp.float32)
    state = lax.fori_loop(
        0, cells, cell, (one, zero, one, zero, zero, one, zero, zero, zero)
    )
    for g in range(group):
        for q in range(9):
            mine[g, q] = state[q][g * part:(g + 1) * part]

    def to_owner(step):
        peer = lax.rem(inner + step, group)
        return pltpu.make_async_remote_copy(
            src_ref=mine.at[peer], dst_ref=maps.at[inner],
            send_sem=a_send.at[peer], recv_sem=a_recv.at[inner],
            device_id={"flow": outer * group + peer}, device_id_type=MESH,
        )

    def from_member(step):
        peer = lax.rem(inner + step, group)
        return pltpu.make_async_remote_copy(
            src_ref=mine.at[peer], dst_ref=maps.at[peer],
            send_sem=a_send.at[peer], recv_sem=a_recv.at[peer],
            device_id={"flow": outer * group + peer}, device_id_type=MESH,
        )

    for step in range(1, group):
        to_owner(step).start()
    maps[inner] = mine[inner]
    for step in range(1, group):
        from_member(step).wait_recv()

    def map_of(ref, m):
        return tuple(ref[m, q] for q in range(9))

    flux = tuple(inl[k, pl.ds(pl.multiple_of(inner * part, part), part)] for k in range(3))

    def to_group(o):
        return pltpu.make_async_remote_copy(
            src_ref=total, dst_ref=totals.at[outer],
            send_sem=b_send.at[o], recv_sem=b_recv.at[outer],
            device_id={"flow": o * group + inner}, device_id_type=MESH,
        )

    if groups > 1:
        product = map_of(maps, 0)
        for m in range(1, group):
            product = after(map_of(maps, m), product)
        for q in range(9):
            total[q] = product[q]

        for o in range(1, groups):
            @pl.when(outer < o)
            def _():
                to_group(o).start()

        def earlier(o, flux):
            pltpu.make_async_remote_copy(
                src_ref=total, dst_ref=totals.at[o],
                send_sem=b_send.at[o], recv_sem=b_recv.at[o],
                device_id={"flow": o * group + inner}, device_id_type=MESH,
            ).wait_recv()
            return apply_map(map_of(totals, o), flux)

        flux = lax.fori_loop(0, outer, earlier, flux)

    for m in range(group):
        for k in range(3):
            fluxes[m, k] = flux[k]
        if m < group - 1:
            flux = apply_map(map_of(maps, m), flux)

    def to_member(step):
        peer = lax.rem(inner + step, group)
        return pltpu.make_async_remote_copy(
            src_ref=fluxes.at[peer], dst_ref=entering.at[inner],
            send_sem=c_send.at[peer], recv_sem=c_recv.at[inner],
            device_id={"flow": outer * group + peer}, device_id_type=MESH,
        )

    def from_owner(step):
        peer = lax.rem(inner + step, group)
        return pltpu.make_async_remote_copy(
            src_ref=fluxes.at[peer], dst_ref=entering.at[peer],
            send_sem=c_send.at[peer], recv_sem=c_recv.at[peer],
            device_id={"flow": outer * group + peer}, device_id_type=MESH,
        )

    for step in range(1, group):
        to_member(step).start()
    entering[inner] = fluxes[inner]
    for step in range(1, group):
        from_owner(step).wait_recv()

    q = [jnp.concatenate([entering[g, k] for g in range(group)], axis=0) for k in range(3)]

    def finish(i, carry):
        fresh = apply_map(tuple(local[n, i] for n in range(9)), q)
        for k in range(3):
            out[k, i] = fresh[k]
        return carry

    lax.fori_loop(0, cells, finish, 0)

    for step in range(1, group):
        to_owner(step).wait_send()
        to_member(step).wait_send()
    for o in range(1, groups):
        @pl.when(outer < o)
        def _():
            to_group(o).wait_send()

    @pl.when(lat < lats - 1)
    def _():
        to_high.wait_send()

    @pl.when(lat > 0)
    def _():
        to_low.wait_send()


def per_device(flows, lats, concentration, courant, rates, spread, inlet):
    _, cells, rows, width = concentration.shape
    group = GROUP
    groups = flows // group
    part = rows // group
    f32 = jnp.float32
    dma = pltpu.SemaphoreType.DMA
    return pl.pallas_call(
        functools.partial(kernel, groups, group, lats),
        out_shape=jax.ShapeDtypeStruct(concentration.shape, f32),
        in_specs=[pl.BlockSpec(memory_space=pltpu.HBM)] * 5,
        out_specs=pl.BlockSpec(memory_space=pltpu.VMEM),
        scratch_shapes=[
            pltpu.VMEM((3, cells, rows + 2 * EDGE, width), f32),
            pltpu.VMEM((3, cells, rows, width), f32),
            pltpu.VMEM((2, cells, rows, width), f32),
            pltpu.VMEM((rows, width), f32),
            pltpu.VMEM((3, rows, width), f32),
            pltpu.VMEM((9, cells, rows, width), f32),
            pltpu.VMEM((group, 9, part, width), f32),
            pltpu.VMEM((group, 9, part, width), f32),
            pltpu.VMEM((9, part, width), f32),
            pltpu.VMEM((groups, 9, part, width), f32),
            pltpu.VMEM((group, 3, part, width), f32),
            pltpu.VMEM((group, 3, part, width), f32),
            dma((5,)), dma((2,)), dma((2,)),
            dma((group,)), dma((group,)),
            dma((groups,)), dma((groups,)),
            dma((group,)), dma((group,)),
        ],
        compiler_params=pltpu.CompilerParams(
            collective_id=0, has_side_effects=True, vmem_limit_bytes=24 * 2**20
        ),
        cost_estimate=pl.CostEstimate(
            flops=100 * cells * rows * width, bytes_accessed=44 * cells * rows * width,
            transcendentals=0,
        ),
    )(concentration, courant, rates, spread, inlet)


def solution(mesh):
    in_specs = (
        P(None, "flow", "lat", None),
        P(None, "flow", "lat", None),
        P(None, "flow", "lat", None),
        P("lat", None),
        P(None, "lat", None),
    )
    out_specs = P(None, "flow", "lat", None)
    body = functools.partial(per_device, mesh.shape["flow"], mesh.shape["lat"])
    return jax.shard_map(
        body, mesh=mesh, in_specs=in_specs, out_specs=out_specs, check_vma=False
    )
```

time: 132 us -> 23.8 us (0.18)
  the two profiles are of different devices: /device:TPU:8 before, /device:TPU:24 now
where the time goes in v1:
time: 23.8 us; the launch traced here: 23.5 us
  Pallas kernels  17.8 us (75%)
  local copies, waits for them, and re-layouts  5.7 us (24%)
    pallas_call x1, Pallas kernels, per_device(): pl.pallas_call(functools.partial(kernel, groups, group, lats), out_shape=...  17.8 us
    unnamed x11, local copies, waits for them, and re-layouts  5.7 us

profile of v1, /device:TPU:24, one launch (start us, length us, event | category | flops | bytes accessed | tf_op | source)
XLA Modules:
  0.0 23.5 jit_solution(5982326112529282683)
XLA Ops:
  0.0 0.0 copy-start
  0.0 1.1 %copy-done = f32[3,16,32,128]{3,2,1,0:T(8,128)S(1)} copy-done((f32[3,16,32,128]{3,2,1,0:T(8,128)S(1)}, f32[3,16,32,128]{3,2,1,0:T(8,128)}, u32[]{:S(2)}) %copy-start) | copy-done | bytes 786456
  1.1 0.0 copy-start.1
  1.1 1.1 %copy-done.1 = f32[3,16,32,128]{3,2,1,0:T(8,128)S(1)} copy-done((f32[3,16,32,128]{3,2,1,0:T(8,128)S(1)}, f32[3,16,32,128]{3,2,1,0:T(8,128)}, u32[]{:S(2)}) %copy-start.1) | copy-done | bytes 786456
  2.3 0.0 copy-start.2
  2.3 1.0 %copy-done.2 = f32[2,16,32,128]{3,2,1,0:T(8,128)S(1)} copy-done((f32[2,16,32,128]{3,2,1,0:T(8,128)S(1)}, f32[2,16,32,128]{3,2,1,0:T(8,128)}, u32[]{:S(2)}) %copy-start.2) | copy-done | bytes 524312
  3.3 0.0 copy-start.3
  3.3 0.8 %copy-done.3 = f32[3,32,128]{2,1,0:T(8,128)S(1)} copy-done((f32[3,32,128]{2,1,0:T(8,128)S(1)}, f32[3,32,128]{2,1,0:T(8,128)}, u32[]{:S(2)}) %copy-start.3) | copy-done | bytes 49176
  4.1 0.0 copy-start.4
  4.1 0.7 %copy-done.4 = f32[32,128]{1,0:T(8,128)S(1)} copy-done((f32[32,128]{1,0:T(8,128)S(1)}, f32[32,128]{1,0:T(8,128)}, u32[]{:S(2)}) %copy-start.4) | copy-done | bytes 16408
  4.8 17.8 %shard_map.55 = f32[3,16,32,128]{3,2,1,0:T(8,128)S(1)} custom-call(f32[3,16,32,128]{3,2,1,0:T(8,128)S(1)} %copy-done, f32[3,16,32,128]{3,2,1,0:T(8,128)S(1)} %copy-done.1, f32[2,16,32,128]{3,2,1,0:T(8,128)S(1)} %copy-done.2, f32[32,128]{1,0:T(8,128)S(1)} %copy-done.4, f32[3,32,128]{2,1,0:T(8,128)S(1)} %copy-done.3), custom_call_target="tpu_custom_call" | custom-call | flops 6553600 | bytes 2883584 | tf_op jit(solution)/shard_map/pallas_call | solution.py:273
  22.6 0.9 %copy.7 = f32[3,16,32,128]{3,2,1,0:T(8,128)} copy(f32[3,16,32,128]{3,2,1,0:T(8,128)S(1)} %shard_map.55) | data formatting | bytes 1572864
Async XLA Ops:
  0.0 1.1 %copy-start = (f32[3,16,32,128]{3,2,1,0:T(8,128)S(1)}, f32[3,16,32,128]{3,2,1,0:T(8,128)}, u32[]{:S(2)}) copy-start(f32[3,16,32,128]{3,2,1,0:T(8,128)} %conc.1) | copy-start | bytes 2359300
  1.1 1.1 %copy-start.1 = (f32[3,16,32,128]{3,2,1,0:T(8,128)S(1)}, f32[3,16,32,128]{3,2,1,0:T(8,128)}, u32[]{:S(2)}) copy-start(f32[3,16,32,128]{3,2,1,0:T(8,128)} %courant.1) | copy-start | bytes 2359300
  2.3 1.0 %copy-start.2 = (f32[2,16,32,128]{3,2,1,0:T(8,128)S(1)}, f32[2,16,32,128]{3,2,1,0:T(8,128)}, u32[]{:S(2)}) copy-start(f32[2,16,32,128]{3,2,1,0:T(8,128)} %rates.1) | copy-start | bytes 1572868
  3.3 0.8 %copy-start.3 = (f32[3,32,128]{2,1,0:T(8,128)S(1)}, f32[3,32,128]{2,1,0:T(8,128)}, u32[]{:S(2)}) copy-start(f32[3,32,128]{2,1,0:T(8,128)} %inlet.1) | copy-start | bytes 147460
  4.1 0.7 %copy-start.4 = (f32[32,128]{1,0:T(8,128)S(1)}, f32[32,128]{1,0:T(8,128)}, u32[]{:S(2)}) copy-start(f32[32,128]{1,0:T(8,128)} %spread.1) | copy-start | bytes 49156

commit v2 on v1

v2 whole, which is shorter than its diff:
```python
import functools
import jax
import jax.numpy as jnp
from jax import lax
from jax.experimental import pallas as pl
from jax.experimental.pallas import tpu as pltpu
from jax.sharding import PartitionSpec as P

MESH = pl.DeviceIdType.MESH
GROUP = 4
EDGE = 8
UNROLL = 16


def apply_map(m, q):
    return (
        m[0] * q[0] + m[6],
        m[1] * q[0] + m[2] * q[1] + m[7],
        m[3] * q[0] + m[4] * q[1] + m[5] * q[2] + m[8],
    )


def times(m, n):
    return (
        m[0] * n[0],
        m[1] * n[0] + m[2] * n[1],
        m[2] * n[2],
        m[3] * n[0] + m[4] * n[1] + m[5] * n[3],
        m[4] * n[2] + m[5] * n[4],
        m[5] * n[5],
    )


def inverse(x):
    rough = pl.reciprocal(x, approx=True)
    return rough * (2.0 - x * rough)


def kernel(
    groups, group, lats,
    conc, courant, rates, spread, inlet, out,
    pad, cour, rate, spr, inl, local, inv, mine, maps, total, totals, fluxes, entering,
    load_sem, tile_sem, halo_send, halo_recv,
    a_send, a_recv, o_send, o_recv, b_send, b_recv, p_send, p_recv, c_send, c_recv,
):
    cells, rows, width = cour.shape[1:]
    part = rows // group
    tile = max(part, EDGE)
    owners = tile // part
    tiles = rows // tile
    flow = lax.axis_index("flow")
    lat = lax.axis_index("lat")
    inner = lax.rem(flow, group)
    outer = lax.div(flow, group)
    not_low, not_high = lat > 0, lat < lats - 1

    def tile_at(step):
        return lax.rem(lax.div(inner, owners) + step, tiles)

    def rows_of(t):
        return pl.ds(pl.multiple_of(t * tile, tile), tile)

    order = [tile_at(step) for step in range(1, tiles)] + [tile_at(0)]
    tile_loads = []
    for n, t in enumerate(order):
        at = rows_of(t)
        tile_loads.append([
            pltpu.make_async_copy(courant.at[:, :, at], cour.at[:, :, at], tile_sem.at[0, n]),
            pltpu.make_async_copy(rates.at[:, :, at], rate.at[:, :, at], tile_sem.at[1, n]),
        ])
    loads = [
        pltpu.make_async_copy(src, dst, load_sem.at[i])
        for i, (src, dst) in enumerate((
            (conc, pad.at[:, :, EDGE:EDGE + rows]), (spread, spr), (inlet, inl),
        ))
    ]
    for load in sum(tile_loads, []) + loads:
        load.start()

    barrier = pltpu.get_barrier_semaphore()
    for step in range(1, group):
        peer = outer * group + lax.rem(inner + step, group)
        pl.semaphore_signal(barrier, inc=1, device_id={"flow": peer}, device_id_type=MESH)
    for step in range(1, groups):
        peer = lax.rem(outer + step, groups) * group + inner
        pl.semaphore_signal(barrier, inc=1, device_id={"flow": peer}, device_id_type=MESH)

    @pl.when(not_low)
    def _():
        pl.semaphore_signal(barrier, inc=1, device_id={"lat": lat - 1}, device_id_type=MESH)

    @pl.when(not_high)
    def _():
        pl.semaphore_signal(barrier, inc=1, device_id={"lat": lat + 1}, device_id_type=MESH)

    nothing = jnp.zeros((3, cells, EDGE, width), jnp.float32)

    @pl.when(lat == 0)
    def _():
        pad[:, :, 0:EDGE] = nothing

    @pl.when(lat == lats - 1)
    def _():
        pad[:, :, EDGE + rows:2 * EDGE + rows] = nothing

    beside = jnp.where(not_low, 1, 0) + jnp.where(not_high, 1, 0)
    pl.semaphore_wait(barrier, group - 1 + groups - 1 + beside)

    to_high = pltpu.make_async_remote_copy(
        src_ref=conc.at[:, :, rows - EDGE:rows], dst_ref=pad.at[:, :, 0:EDGE],
        send_sem=halo_send.at[0], recv_sem=halo_recv.at[0],
        device_id={"lat": lat + 1}, device_id_type=MESH,
    )
    to_low = pltpu.make_async_remote_copy(
        src_ref=conc.at[:, :, 0:EDGE], dst_ref=pad.at[:, :, EDGE + rows:2 * EDGE + rows],
        send_sem=halo_send.at[1], recv_sem=halo_recv.at[1],
        device_id={"lat": lat - 1}, device_id_type=MESH,
    )

    @pl.when(not_high)
    def _():
        to_high.start()

    @pl.when(not_low)
    def _():
        to_low.start()

    matrix, offset = slice(0, 6), slice(6, 9)

    def between(src, dst, there, send, recv, slot, cut, peer, arriving):
        lands = peer if arriving else slot
        return pltpu.make_async_remote_copy(
            src_ref=src.at[peer, cut], dst_ref=dst.at[lands, cut],
            send_sem=send.at[peer], recv_sem=recv.at[lands],
            device_id={"flow": there(peer)}, device_id_type=MESH,
        )

    def member(peer):
        return outer * group + peer

    def matrix_copy(peer, arriving=False):
        return between(mine, maps, member, a_send, a_recv, inner, matrix, peer, arriving)

    def offset_copy(peer, arriving=False):
        return between(mine, maps, member, o_send, o_recv, inner, offset, peer, arriving)

    def flux_copy(peer, arriving=False):
        return between(fluxes, entering, member, c_send, c_recv, inner, slice(0, 3), peer, arriving)

    def put(t, last, values, first, copy):
        for j in range(owners):
            peer = t * owners + j
            for q, value in enumerate(values):
                mine[peer, first + q] = value[j * part:(j + 1) * part]
            if last:
                @pl.when(peer != inner)
                def _():
                    copy(peer).start()
            else:
                copy(peer).start()

    one = jnp.ones((tile, width), jnp.float32)
    zero = jnp.zeros((tile, width), jnp.float32)

    for n, t in enumerate(order):
        for load in tile_loads[n]:
            load.wait()
        at = rows_of(t)

        def matrix_cell(i, state, at=at):
            m00, m10, m11, m20, m21, m22 = state
            c0, c1, c2 = cour[0, i, at], cour[1, i, at], cour[2, i, at]
            k0, k1 = rate[0, i, at], rate[1, i, at]
            r0, r1, r2 = inverse(1.0 + c0 + k0), inverse(1.0 + c1 + k1), inverse(1.0 + c2)
            for k, r in enumerate((r0, r1, r2)):
                inv[k, i, at] = r
            u00 = m00 * r0
            u10 = (m10 + k0 * u00) * r1
            u20 = (m20 + k1 * u10) * r2
            u11 = m11 * r1
            u21 = (m21 + k1 * u11) * r2
            u22 = m22 * r2
            for q, value in enumerate((u00, u10, u11, u20, u21, u22)):
                local[q, i, at] = value
            return c0 * u00, c1 * u10, c1 * u11, c2 * u20, c2 * u21, c2 * u22

        state = lax.fori_loop(
            0, cells, matrix_cell, (one, zero, one, zero, zero, one), unroll=UNROLL
        )
        put(t, n == tiles - 1, state, 0, matrix_copy)

    for load in loads:
        load.wait()

    @pl.when(not_low)
    def _():
        to_high.wait_recv()

    @pl.when(not_high)
    def _():
        to_low.wait_recv()

    lane = lax.broadcasted_iota(jnp.int32, (tile, width), 1)
    first, last = lane == 0, lane == width - 1

    for n, t in enumerate(order):
        at = rows_of(t)
        scale = spr[at]

        def source(k, i, t=t, scale=scale):
            mid = pad[k, i, pl.ds(pl.multiple_of(t * tile + EDGE, EDGE), tile)]
            left = jnp.where(first, 0.0, pltpu.roll(mid, 1, 1))
            right = jnp.where(last, 0.0, pltpu.roll(mid, width - 1, 1))
            up = pad[k, i, pl.ds(t * tile + EDGE - 1, tile)]
            down = pad[k, i, pl.ds(t * tile + EDGE + 1, tile)]
            return mid + scale * (up + down + left + right - 4.0 * mid)

        def offset_cell(i, state, at=at, source=source):
            w0, w1, w2 = state
            v0 = (source(0, i) + w0) * inv[0, i, at]
            v1 = (source(1, i) + w1 + rate[0, i, at] * v0) * inv[1, i, at]
            v2 = (source(2, i) + w2 + rate[1, i, at] * v1) * inv[2, i, at]
            for k, value in enumerate((v0, v1, v2)):
                local[6 + k, i, at] = value
            return cour[0, i, at] * v0, cour[1, i, at] * v1, cour[2, i, at] * v2

        state = lax.fori_loop(0, cells, offset_cell, (zero, zero, zero), unroll=UNROLL)
        put(t, n == tiles - 1, state, 6, offset_copy)

    maps[inner] = mine[inner]

    def map_of(ref, m):
        return tuple(ref[m, q] for q in range(9))

    def group_copy(o, cut, send, recv, arriving):
        lands = o if arriving else outer
        return pltpu.make_async_remote_copy(
            src_ref=total.at[cut], dst_ref=totals.at[lands, cut],
            send_sem=send.at[o], recv_sem=recv.at[lands],
            device_id={"flow": o * group + inner}, device_id_type=MESH,
        )

    def total_matrix(o, arriving=False):
        return group_copy(o, matrix, b_send, b_recv, arriving)

    def total_offset(o, arriving=False):
        return group_copy(o, offset, p_send, p_recv, arriving)

    def to_later(copy):
        for o in reversed(range(1, groups)):
            @pl.when(outer < o)
            def _():
                copy(o).start()

    peers = [lax.rem(inner + step, group) for step in range(1, group)]
    for peer in peers:
        matrix_copy(peer, True).wait_recv()
    if groups > 1:
        product = tuple(maps[0, q] for q in range(6))
        for m in range(1, group):
            product = times(tuple(maps[m, q] for q in range(6)), product)
        for q in range(6):
            total[q] = product[q]
        to_later(total_matrix)
    for peer in peers:
        offset_copy(peer, True).wait_recv()

    flux = tuple(inl[k, pl.ds(pl.multiple_of(inner * part, part), part)] for k in range(3))
    if groups > 1:
        shift = tuple(maps[0, q] for q in range(6, 9))
        for m in range(1, group):
            shift = apply_map(map_of(maps, m), shift)
        for k in range(3):
            total[6 + k] = shift[k]
        to_later(total_offset)

        def earlier(o, flux):
            total_matrix(o, True).wait_recv()
            total_offset(o, True).wait_recv()
            return apply_map(map_of(totals, o), flux)

        flux = lax.fori_loop(0, outer, earlier, flux)

    for m in range(group):
        for k in range(3):
            fluxes[m, k] = flux[k]
        if m < group - 1:
            flux = apply_map(map_of(maps, m), flux)
    for peer in peers:
        flux_copy(peer).start()
    entering[inner] = fluxes[inner]

    for step in range(tiles):
        t = tile_at(step)
        at = rows_of(t)
        for j in range(owners):
            peer = t * owners + j
            if step:
                flux_copy(peer, True).wait_recv()
            else:
                @pl.when(peer != inner)
                def _():
                    flux_copy(peer, True).wait_recv()
        q = [
            jnp.concatenate([entering[t * owners + j, k] for j in range(owners)], axis=0)
            for k in range(3)
        ]

        def finish(i, carry, at=at, q=q):
            fresh = apply_map(tuple(local[n, i, at] for n in range(9)), q)
            for k in range(3):
                out[k, i, at] = fresh[k]
            return carry

        lax.fori_loop(0, cells, finish, 0, unroll=UNROLL)

    for peer in peers:
        matrix_copy(peer).wait_send()
        offset_copy(peer).wait_send()
        flux_copy(peer).wait_send()
    for o in range(1, groups):
        @pl.when(outer < o)
        def _():
            total_matrix(o).wait_send()
            total_offset(o).wait_send()

    @pl.when(not_high)
    def _():
        to_high.wait_send()

    @pl.when(not_low)
    def _():
        to_low.wait_send()


def per_device(flows, lats, concentration, courant, rates, spread, inlet):
    _, cells, rows, width = concentration.shape
    group = GROUP
    groups = flows // group
    part = rows // group
    f32 = jnp.float32
    dma = pltpu.SemaphoreType.DMA
    return pl.pallas_call(
        functools.partial(kernel, groups, group, lats),
        out_shape=jax.ShapeDtypeStruct(concentration.shape, f32),
        in_specs=[pl.BlockSpec(memory_space=pltpu.HBM)] * 5,
        out_specs=pl.BlockSpec(memory_space=pltpu.VMEM),
        scratch_shapes=[
            pltpu.VMEM((3, cells, rows + 2 * EDGE, width), f32),
            pltpu.VMEM((3, cells, rows, width), f32),
            pltpu.VMEM((2, cells, rows, width), f32),
            pltpu.VMEM((rows, width), f32),
            pltpu.VMEM((3, rows, width), f32),
            pltpu.VMEM((9, cells, rows, width), f32),
            pltpu.VMEM((3, cells, rows, width), f32),
            pltpu.VMEM((group, 9, part, width), f32),
            pltpu.VMEM((group, 9, part, width), f32),
            pltpu.VMEM((9, part, width), f32),
            pltpu.VMEM((groups, 9, part, width), f32),
            pltpu.VMEM((group, 3, part, width), f32),
            pltpu.VMEM((group, 3, part, width), f32),
            dma((3,)), dma((2, rows // max(part, EDGE))), dma((2,)), dma((2,)),
            dma((group,)), dma((group,)), dma((group,)), dma((group,)),
            dma((groups,)), dma((groups,)), dma((groups,)), dma((groups,)),
            dma((group,)), dma((group,)),
        ],
        compiler_params=pltpu.CompilerParams(
            collective_id=0, has_side_effects=True, vmem_limit_bytes=24 * 2**20
        ),
        cost_estimate=pl.CostEstimate(
            flops=100 * cells * rows * width, bytes_accessed=44 * cells * rows * width,
            transcendentals=0,
        ),
    )(*(
        pltpu.with_memory_space_constraint(array, pltpu.HBM)
        for array in (concentration, courant, rates, spread, inlet)
    ))


def solution(mesh):
    in_specs = (
        P(None, "flow", "lat", None),
        P(None, "flow", "lat", None),
        P(None, "flow", "lat", None),
        P("lat", None),
        P(None, "lat", None),
    )
    out_specs = P(None, "flow", "lat", None)
    body = functools.partial(per_device, mesh.shape["flow"], mesh.shape["lat"])
    return jax.shard_map(
        body, mesh=mesh, in_specs=in_specs, out_specs=out_specs, check_vma=False
    )
```

time: 23.8 us -> 16.1 us (0.68)
  the two profiles are of different devices: /device:TPU:24 before, /device:TPU:8 now
where the time goes in v2:
time: 16.1 us; the launch traced here: 16 us
  Pallas kernels  15.1 us (94%)
  local copies, waits for them, and re-layouts  0.88 us (5%)
    pallas_call x1, Pallas kernels, per_device(): pl.pallas_call(functools.partial(kernel, groups, group, lats), out_shape=...  15.1 us
    unnamed x1, local copies, waits for them, and re-layouts  0.88 us

profile of v2, /device:TPU:8, one launch (start us, length us, event | category | flops | bytes accessed | tf_op | source)
XLA Modules:
  0.0 16.0 jit_solution(2465205833709951935)
XLA Ops:
  0.0 15.1 %shard_map.55 = f32[3,16,32,128]{3,2,1,0:T(8,128)S(1)} custom-call(f32[3,16,32,128]{3,2,1,0:T(8,128)} %conc.1, f32[3,16,32,128]{3,2,1,0:T(8,128)} %courant.1, f32[2,16,32,128]{3,2,1,0:T(8,128)} %rates.1, f32[32,128]{1,0:T(8,128)} %spread.1, f32[3,32,128]{2,1,0:T(8,128)} %inlet.1), custom_call_target="tpu_custom_call" | custom-call | flops 6553600 | bytes 2883584 | tf_op jit(solution)/shard_map/pallas_call | solution.py:343
  15.1 0.9 %copy.7 = f32[3,16,32,128]{3,2,1,0:T(8,128)} copy(f32[3,16,32,128]{3,2,1,0:T(8,128)S(1)} %shard_map.55) | data formatting | bytes 1572864

commit v3 on v2

--- a/solution.py
+++ b/solution.py
@@ -74,9 +74,6 @@
             (conc, pad.at[:, :, EDGE:EDGE + rows]), (spread, spr), (inlet, inl),
         ))
     ]
-    for load in sum(tile_loads, []) + loads:
-        load.start()
-
     barrier = pltpu.get_barrier_semaphore()
     for step in range(1, group):
         peer = outer * group + lax.rem(inner + step, group)
@@ -93,6 +90,9 @@
     def _():
         pl.semaphore_signal(barrier, inc=1, device_id={"lat": lat + 1}, device_id_type=MESH)
 
+    for load in sum(tile_loads, []) + loads:
+        load.start()
+
     nothing = jnp.zeros((3, cells, EDGE, width), jnp.float32)
 
     @pl.when(lat == 0)
@@ -107,12 +107,12 @@
     pl.semaphore_wait(barrier, group - 1 + groups - 1 + beside)
 
     to_high = pltpu.make_async_remote_copy(
-        src_ref=conc.at[:, :, rows - EDGE:rows], dst_ref=pad.at[:, :, 0:EDGE],
+        src_ref=conc.at[:, :, rows - 1:rows], dst_ref=pad.at[:, :, EDGE - 1:EDGE],
         send_sem=halo_send.at[0], recv_sem=halo_recv.at[0],
         device_id={"lat": lat + 1}, device_id_type=MESH,
     )
     to_low = pltpu.make_async_remote_copy(
-        src_ref=conc.at[:, :, 0:EDGE], dst_ref=pad.at[:, :, EDGE + rows:2 * EDGE + rows],
+        src_ref=conc.at[:, :, 0:1], dst_ref=pad.at[:, :, EDGE + rows:EDGE + rows + 1],
         send_sem=halo_send.at[1], recv_sem=halo_recv.at[1],
         device_id={"lat": lat - 1}, device_id_type=MESH,
     )

time: 16.1 us -> 15.9 us (0.988)
  Pallas kernels: 15.1 us -> 14.9 us
    pallas_call x1, Pallas kernels: 15.1 us -> 14.9 us  [per_device(): pl.pallas_call(functools.partial(kernel, groups, group, lats), out_shape=...]
where the time goes in v3:
time: 15.9 us; the launch traced here: 15.8 us
  Pallas kernels  14.9 us (94%)
  local copies, waits for them, and re-layouts  0.88 us (6%)
    pallas_call x1, Pallas kernels, per_device(): pl.pallas_call(functools.partial(kernel, groups, group, lats), out_shape=...  14.9 us
    unnamed x1, local copies, waits for them, and re-layouts  0.88 us

profile of v3, /device:TPU:8, one launch (start us, length us, event | category | flops | bytes accessed | tf_op | source)
XLA Modules:
  0.0 15.8 jit_solution(10489674155773328993)
XLA Ops:
  0.0 14.9 %shard_map.55 = f32[3,16,32,128]{3,2,1,0:T(8,128)S(1)} custom-call(f32[3,16,32,128]{3,2,1,0:T(8,128)} %conc.1, f32[3,16,32,128]{3,2,1,0:T(8,128)} %courant.1, f32[2,16,32,128]{3,2,1,0:T(8,128)} %rates.1, f32[32,128]{1,0:T(8,128)} %spread.1, f32[3,32,128]{2,1,0:T(8,128)} %inlet.1), custom_call_target="tpu_custom_call" | custom-call | flops 6553600 | bytes 2883584 | tf_op jit(solution)/shard_map/pallas_call | solution.py:343
  14.9 0.9 %copy.7 = f32[3,16,32,128]{3,2,1,0:T(8,128)} copy(f32[3,16,32,128]{3,2,1,0:T(8,128)S(1)} %shard_map.55) | data formatting | bytes 1572864

commit v4 on v3

--- a/solution.py
+++ b/solution.py
@@ -7,7 +7,7 @@
 from jax.sharding import PartitionSpec as P
 
 MESH = pl.DeviceIdType.MESH
-GROUP = 4
+GROUP = 16
 EDGE = 8
 UNROLL = 16
 

time: 15.9 us -> 19.8 us (1.25)
  the two profiles are of different devices: /device:TPU:8 before, /device:TPU:0 now
where the time goes in v4:
time: 19.8 us; the launch traced here: 19.7 us
  Pallas kernels  18.8 us (95%)
  local copies, waits for them, and re-layouts  0.88 us (4%)
    pallas_call x1, Pallas kernels, per_device(): pl.pallas_call(functools.partial(kernel, groups, group, lats), out_shape=...  18.8 us
    unnamed x1, local copies, waits for them, and re-layouts  0.88 us

profile of v4, /device:TPU:0, one launch (start us, length us, event | category | flops | bytes accessed | tf_op | source)
XLA Modules:
  0.0 19.7 jit_solution(10544716958503356566)
XLA Ops:
  0.0 18.8 %shard_map.55 = f32[3,16,32,128]{3,2,1,0:T(8,128)S(1)} custom-call(f32[3,16,32,128]{3,2,1,0:T(8,128)} %conc.1, f32[3,16,32,128]{3,2,1,0:T(8,128)} %courant.1, f32[2,16,32,128]{3,2,1,0:T(8,128)} %rates.1, f32[32,128]{1,0:T(8,128)} %spread.1, f32[3,32,128]{2,1,0:T(8,128)} %inlet.1), custom_call_target="tpu_custom_call" | custom-call | flops 6553600 | bytes 2883584 | tf_op jit(solution)/shard_map/pallas_call | solution.py:343
  18.8 0.9 %copy.7 = f32[3,16,32,128]{3,2,1,0:T(8,128)} copy(f32[3,16,32,128]{3,2,1,0:T(8,128)S(1)} %shard_map.55) | data formatting | bytes 1572864

commit v5 on v3

--- a/solution.py
+++ b/solution.py
@@ -60,14 +60,16 @@
     def rows_of(t):
         return pl.ds(pl.multiple_of(t * tile, tile), tile)
 
-    order = [tile_at(step) for step in range(1, tiles)] + [tile_at(0)]
-    tile_loads = []
-    for n, t in enumerate(order):
-        at = rows_of(t)
-        tile_loads.append([
+    def nth(n):
+        return tile_at(n + 1)
+
+    def tile_loads(n):
+        at = rows_of(nth(n))
+        return (
             pltpu.make_async_copy(courant.at[:, :, at], cour.at[:, :, at], tile_sem.at[0, n]),
             pltpu.make_async_copy(rates.at[:, :, at], rate.at[:, :, at], tile_sem.at[1, n]),
-        ])
+        )
+
     loads = [
         pltpu.make_async_copy(src, dst, load_sem.at[i])
         for i, (src, dst) in enumerate((
@@ -90,7 +92,10 @@
     def _():
         pl.semaphore_signal(barrier, inc=1, device_id={"lat": lat + 1}, device_id_type=MESH)
 
-    for load in sum(tile_loads, []) + loads:
+    for n in range(tiles):
+        for load in tile_loads(n):
+            load.start()
+    for load in loads:
         load.start()
 
     nothing = jnp.zeros((3, cells, EDGE, width), jnp.float32)
@@ -147,27 +152,26 @@
     def flux_copy(peer, arriving=False):
         return between(fluxes, entering, member, c_send, c_recv, inner, slice(0, 3), peer, arriving)
 
-    def put(t, last, values, first, copy):
+    def put(t, values, first, copy):
         for j in range(owners):
             peer = t * owners + j
             for q, value in enumerate(values):
                 mine[peer, first + q] = value[j * part:(j + 1) * part]
-            if last:
-                @pl.when(peer != inner)
-                def _():
-                    copy(peer).start()
-            else:
+
+            @pl.when(peer != inner)
+            def _():
                 copy(peer).start()
 
     one = jnp.ones((tile, width), jnp.float32)
     zero = jnp.zeros((tile, width), jnp.float32)
 
-    for n, t in enumerate(order):
-        for load in tile_loads[n]:
+    def matrix_tile(n, carry):
+        for load in tile_loads(n):
             load.wait()
+        t = nth(n)
         at = rows_of(t)
 
-        def matrix_cell(i, state, at=at):
+        def matrix_cell(i, state):
             m00, m10, m11, m20, m21, m22 = state
             c0, c1, c2 = cour[0, i, at], cour[1, i, at], cour[2, i, at]
             k0, k1 = rate[0, i, at], rate[1, i, at]
@@ -187,7 +191,10 @@
         state = lax.fori_loop(
             0, cells, matrix_cell, (one, zero, one, zero, zero, one), unroll=UNROLL
         )
-        put(t, n == tiles - 1, state, 0, matrix_copy)
+        put(t, state, 0, matrix_copy)
+        return carry
+
+    lax.fori_loop(0, tiles, matrix_tile, 0)
 
     for load in loads:
         load.wait()
@@ -203,11 +210,50 @@
     lane = lax.broadcasted_iota(jnp.int32, (tile, width), 1)
     first, last = lane == 0, lane == width - 1
 
-    for n, t in enumerate(order):
+    def group_copy(o, cut, send, recv, arriving):
+        lands = o if arriving else outer
+        return pltpu.make_async_remote_copy(
+            src_ref=total.at[cut], dst_ref=totals.at[lands, cut],
+            send_sem=send.at[o], recv_sem=recv.at[lands],
+            device_id={"flow": o * group + inner}, device_id_type=MESH,
+        )
+
+    def total_matrix(o, arriving=False):
+        return group_copy(o, matrix, b_send, b_recv, arriving)
+
+    def total_offset(o, arriving=False):
+        return group_copy(o, offset, p_send, p_recv, arriving)
+
+    peers = [lax.rem(inner + step, group) for step in range(1, group)]
+
+    def fold_matrices():
+        maps[inner, matrix] = mine[inner, matrix]
+        for peer in peers:
+            matrix_copy(peer, True).wait_recv()
+
+        if groups > 2:
+            @pl.when((outer > 0) & (outer < groups - 1))
+            def _():
+                product = tuple(maps[0, q] for q in range(6))
+                for m in range(1, group):
+                    product = times(tuple(maps[m, q] for q in range(6)), product)
+                for q in range(6):
+                    total[q] = product[q]
+                for o in reversed(range(2, groups)):
+                    @pl.when(outer < o)
+                    def _():
+                        total_matrix(o).start()
+
+    def offset_tile(n, carry):
+        @pl.when(n == tiles - 1)
+        def _():
+            fold_matrices()
+
+        t = nth(n)
         at = rows_of(t)
         scale = spr[at]
 
-        def source(k, i, t=t, scale=scale):
+        def source(k, i):
             mid = pad[k, i, pl.ds(pl.multiple_of(t * tile + EDGE, EDGE), tile)]
             left = jnp.where(first, 0.0, pltpu.roll(mid, 1, 1))
             right = jnp.where(last, 0.0, pltpu.roll(mid, width - 1, 1))
@@ -215,7 +261,7 @@
             down = pad[k, i, pl.ds(t * tile + EDGE + 1, tile)]
             return mid + scale * (up + down + left + right - 4.0 * mid)
 
-        def offset_cell(i, state, at=at, source=source):
+        def offset_cell(i, state):
             w0, w1, w2 = state
             v0 = (source(0, i) + w0) * inv[0, i, at]
             v1 = (source(1, i) + w1 + rate[0, i, at] * v0) * inv[1, i, at]
@@ -225,94 +271,85 @@
             return cour[0, i, at] * v0, cour[1, i, at] * v1, cour[2, i, at] * v2
 
         state = lax.fori_loop(0, cells, offset_cell, (zero, zero, zero), unroll=UNROLL)
-        put(t, n == tiles - 1, state, 6, offset_copy)
-
-    maps[inner] = mine[inner]
+        put(t, state, 6, offset_copy)
+        return carry
+
+    lax.fori_loop(0, tiles, offset_tile, 0)
 
     def map_of(ref, m):
         return tuple(ref[m, q] for q in range(9))
 
-    def group_copy(o, cut, send, recv, arriving):
-        lands = o if arriving else outer
-        return pltpu.make_async_remote_copy(
-            src_ref=total.at[cut], dst_ref=totals.at[lands, cut],
-            send_sem=send.at[o], recv_sem=recv.at[lands],
-            device_id={"flow": o * group + inner}, device_id_type=MESH,
-        )
-
-    def total_matrix(o, arriving=False):
-        return group_copy(o, matrix, b_send, b_recv, arriving)
-
-    def total_offset(o, arriving=False):
-        return group_copy(o, offset, p_send, p_recv, arriving)
-
-    def to_later(copy):
+    maps[inner, offset] = mine[inner, offset]
+    for peer in peers:
+        offset_copy(peer, True).wait_recv()
+
+    inflow = tuple(inl[k, pl.ds(pl.multiple_of(inner * part, part), part)] for k in range(3))
+    if groups > 1:
+        shift = tuple(jnp.where(outer == 0, value, 0.0) for value in inflow)
+        for m in range(group):
+            shift = apply_map(map_of(maps, m), shift)
+        for k in range(3):
+            total[6 + k] = shift[k]
         for o in reversed(range(1, groups)):
             @pl.when(outer < o)
             def _():
-                copy(o).start()
-
-    peers = [lax.rem(inner + step, group) for step in range(1, group)]
-    for peer in peers:
-        matrix_copy(peer, True).wait_recv()
-    if groups > 1:
-        product = tuple(maps[0, q] for q in range(6))
-        for m in range(1, group):
-            product = times(tuple(maps[m, q] for q in range(6)), product)
-        for q in range(6):
-            total[q] = product[q]
-        to_later(total_matrix)
-    for peer in peers:
-        offset_copy(peer, True).wait_recv()
-
-    flux = tuple(inl[k, pl.ds(pl.multiple_of(inner * part, part), part)] for k in range(3))
-    if groups > 1:
-        shift = tuple(maps[0, q] for q in range(6, 9))
-        for m in range(1, group):
-            shift = apply_map(map_of(maps, m), shift)
-        for k in range(3):
-            total[6 + k] = shift[k]
-        to_later(total_offset)
+                total_offset(o).start()
+
+        @pl.when(outer > 0)
+        def _():
+            total_offset(0, True).wait_recv()
 
         def earlier(o, flux):
             total_matrix(o, True).wait_recv()
             total_offset(o, True).wait_recv()
             return apply_map(map_of(totals, o), flux)
 
-        flux = lax.fori_loop(0, outer, earlier, flux)
-
-    for m in range(group):
+        @pl.when(outer == 0)
+        def _():
+            for k in range(3):
+                fluxes[0, k] = inflow[k]
+
+        @pl.when(outer > 0)
+        def _():
+            flux = lax.fori_loop(1, outer, earlier, tuple(totals[0, 6 + k] for k in range(3)))
+            for k in range(3):
+                fluxes[0, k] = flux[k]
+    else:
+        for k in range(3):
+            fluxes[0, k] = inflow[k]
+
+    flux = tuple(fluxes[0, k] for k in range(3))
+    for m in range(1, group):
+        flux = apply_map(map_of(maps, m - 1), flux)
         for k in range(3):
             fluxes[m, k] = flux[k]
-        if m < group - 1:
-            flux = apply_map(map_of(maps, m), flux)
     for peer in peers:
         flux_copy(peer).start()
     entering[inner] = fluxes[inner]
 
-    for step in range(tiles):
+    def finish_tile(step, carry):
         t = tile_at(step)
         at = rows_of(t)
         for j in range(owners):
             peer = t * owners + j
-            if step:
+
+            @pl.when(peer != inner)
+            def _():
                 flux_copy(peer, True).wait_recv()
-            else:
-                @pl.when(peer != inner)
-                def _():
-                    flux_copy(peer, True).wait_recv()
         q = [
             jnp.concatenate([entering[t * owners + j, k] for j in range(owners)], axis=0)
             for k in range(3)
         ]
 
-        def finish(i, carry, at=at, q=q):
+        def finish(i, carry):
             fresh = apply_map(tuple(local[n, i, at] for n in range(9)), q)
             for k in range(3):
                 out[k, i, at] = fresh[k]
             return carry
 
-        lax.fori_loop(0, cells, finish, 0, unroll=UNROLL)
+        return lax.fori_loop(0, cells, finish, carry, unroll=UNROLL)
+
+    lax.fori_loop(0, tiles, finish_tile, 0)
 
     for peer in peers:
         matrix_copy(peer).wait_send()
@@ -321,8 +358,11 @@
     for o in range(1, groups):
         @pl.when(outer < o)
         def _():
+            total_offset(o).wait_send()
+
+        @pl.when((outer > 0) & (outer < o))
+        def _():
             total_matrix(o).wait_send()
-            total_offset(o).wait_send()
 
     @pl.when(not_high)
     def _():

time: 15.9 us -> 15.3 us (0.962)
  Pallas kernels: 14.9 us -> 14.3 us
    pallas_call x1, Pallas kernels: 14.9 us -> 14.3 us  [per_device(): pl.pallas_call(functools.partial(kernel, groups, group, lats), out_shape=...]
where the time goes in v5:
time: 15.3 us; the launch traced here: 15.2 us
  Pallas kernels  14.3 us (93%)
  local copies, waits for them, and re-layouts  0.88 us (6%)
    pallas_call x1, Pallas kernels, per_device(): pl.pallas_call(functools.partial(kernel, groups, group, lats), out_shape=...  14.3 us
    unnamed x1, local copies, waits for them, and re-layouts  0.88 us

profile of v5, /device:TPU:8, one launch (start us, length us, event | category | flops | bytes accessed | tf_op | source)
XLA Modules:
  0.0 15.2 jit_solution(1402319390994555751)
XLA Ops:
  0.0 14.3 %shard_map.55 = f32[3,16,32,128]{3,2,1,0:T(8,128)S(1)} custom-call(f32[3,16,32,128]{3,2,1,0:T(8,128)} %conc.1, f32[3,16,32,128]{3,2,1,0:T(8,128)} %courant.1, f32[2,16,32,128]{3,2,1,0:T(8,128)} %rates.1, f32[32,128]{1,0:T(8,128)} %spread.1, f32[3,32,128]{2,1,0:T(8,128)} %inlet.1), custom_call_target="tpu_custom_call" | custom-call | flops 6553600 | bytes 2883584 | tf_op jit(solution)/shard_map/pallas_call | solution.py:383
  14.3 0.9 %copy.7 = f32[3,16,32,128]{3,2,1,0:T(8,128)} copy(f32[3,16,32,128]{3,2,1,0:T(8,128)S(1)} %shard_map.55) | data formatting | bytes 1572864

commit v6 on v5

--- a/solution.py
+++ b/solution.py
@@ -199,14 +199,6 @@
     for load in loads:
         load.wait()
 
-    @pl.when(not_low)
-    def _():
-        to_high.wait_recv()
-
-    @pl.when(not_high)
-    def _():
-        to_low.wait_recv()
-
     lane = lax.broadcasted_iota(jnp.int32, (tile, width), 1)
     first, last = lane == 0, lane == width - 1
 
@@ -239,17 +231,23 @@
                     product = times(tuple(maps[m, q] for q in range(6)), product)
                 for q in range(6):
                     total[q] = product[q]
-                for o in reversed(range(2, groups)):
+                for o in range(2, groups):
                     @pl.when(outer < o)
                     def _():
                         total_matrix(o).start()
 
+    last_inside = tiles - 1 - jnp.where(not_low & not_high, 1, 0)
+
     def offset_tile(n, carry):
-        @pl.when(n == tiles - 1)
-        def _():
-            fold_matrices()
-
-        t = nth(n)
+        @pl.when((n == last_inside) & not_low)
+        def _():
+            to_high.wait_recv()
+
+        @pl.when((n == last_inside) & not_high)
+        def _():
+            to_low.wait_recv()
+
+        t = lax.rem(n + jnp.where(not_low, 1, 0), tiles)
         at = rows_of(t)
         scale = spr[at]
 
@@ -275,6 +273,7 @@
         return carry
 
     lax.fori_loop(0, tiles, offset_tile, 0)
+    fold_matrices()
 
     def map_of(ref, m):
         return tuple(ref[m, q] for q in range(9))
@@ -290,7 +289,7 @@
             shift = apply_map(map_of(maps, m), shift)
         for k in range(3):
             total[6 + k] = shift[k]
-        for o in reversed(range(1, groups)):
+        for o in range(1, groups):
             @pl.when(outer < o)
             def _():
                 total_offset(o).start()

time: 15.3 us -> 15.1 us (0.987)
  Pallas kernels: 14.3 us -> 14 us
    pallas_call x1, Pallas kernels: 14.3 us -> 14 us  [per_device(): pl.pallas_call(functools.partial(kernel, groups, group, lats), out_shape=...]
where the time goes in v6:
time: 15.1 us; the launch traced here: 14.9 us
  Pallas kernels  14 us (93%)
  local copies, waits for them, and re-layouts  0.88 us (6%)
    pallas_call x1, Pallas kernels, per_device(): pl.pallas_call(functools.partial(kernel, groups, group, lats), out_shape=...  14 us
    unnamed x1, local copies, waits for them, and re-layouts  0.88 us

profile of v6, /device:TPU:8, one launch (start us, length us, event | category | flops | bytes accessed | tf_op | source)
XLA Modules:
  0.0 14.9 jit_solution(13563466322853533501)
XLA Ops:
  0.0 14.0 %shard_map.55 = f32[3,16,32,128]{3,2,1,0:T(8,128)S(1)} custom-call(f32[3,16,32,128]{3,2,1,0:T(8,128)} %conc.1, f32[3,16,32,128]{3,2,1,0:T(8,128)} %courant.1, f32[2,16,32,128]{3,2,1,0:T(8,128)} %rates.1, f32[32,128]{1,0:T(8,128)} %spread.1, f32[3,32,128]{2,1,0:T(8,128)} %inlet.1), custom_call_target="tpu_custom_call" | custom-call | flops 6553600 | bytes 2883584 | tf_op jit(solution)/shard_map/pallas_call | solution.py:382
  14.0 0.9 %copy.7 = f32[3,16,32,128]{3,2,1,0:T(8,128)} copy(f32[3,16,32,128]{3,2,1,0:T(8,128)S(1)} %shard_map.55) | data formatting | bytes 1572864

commit v7 on v6

--- a/solution.py
+++ b/solution.py
@@ -326,6 +326,26 @@
         flux_copy(peer).start()
     entering[inner] = fluxes[inner]
 
+    for peer in peers:
+        matrix_copy(peer).wait_send()
+        offset_copy(peer).wait_send()
+    for o in range(1, groups):
+        @pl.when(outer < o)
+        def _():
+            total_offset(o).wait_send()
+
+        @pl.when((outer > 0) & (outer < o))
+        def _():
+            total_matrix(o).wait_send()
+
+    @pl.when(not_high)
+    def _():
+        to_high.wait_send()
+
+    @pl.when(not_low)
+    def _():
+        to_low.wait_send()
+
     def finish_tile(step, carry):
         t = tile_at(step)
         at = rows_of(t)
@@ -351,25 +371,7 @@
     lax.fori_loop(0, tiles, finish_tile, 0)
 
     for peer in peers:
-        matrix_copy(peer).wait_send()
-        offset_copy(peer).wait_send()
         flux_copy(peer).wait_send()
-    for o in range(1, groups):
-        @pl.when(outer < o)
-        def _():
-            total_offset(o).wait_send()
-
-        @pl.when((outer > 0) & (outer < o))
-        def _():
-            total_matrix(o).wait_send()
-
-    @pl.when(not_high)
-    def _():
-        to_high.wait_send()
-
-    @pl.when(not_low)
-    def _():
-        to_low.wait_send()
 
 
 def per_device(flows, lats, concentration, courant, rates, spread, inlet):

time: 15.1 us -> 15.1 us (level)
  no operation moved by 1% of the time
where the time goes in v7:
time: 15.1 us; the launch traced here: 14.8 us
  Pallas kernels  14 us (93%)
  local copies, waits for them, and re-layouts  0.88 us (6%)
    pallas_call x1, Pallas kernels, per_device(): pl.pallas_call(functools.partial(kernel, groups, group, lats), out_shape=...  14 us
    unnamed x1, local copies, waits for them, and re-layouts  0.88 us

profile of v7, /device:TPU:8, one launch (start us, length us, event | category | flops | bytes accessed | tf_op | source)
XLA Modules:
  0.0 14.8 jit_solution(8490397617625927866)
XLA Ops:
  0.0 14.0 %shard_map.55 = f32[3,16,32,128]{3,2,1,0:T(8,128)S(1)} custom-call(f32[3,16,32,128]{3,2,1,0:T(8,128)} %conc.1, f32[3,16,32,128]{3,2,1,0:T(8,128)} %courant.1, f32[2,16,32,128]{3,2,1,0:T(8,128)} %rates.1, f32[32,128]{1,0:T(8,128)} %spread.1, f32[3,32,128]{2,1,0:T(8,128)} %inlet.1), custom_call_target="tpu_custom_call" | custom-call | flops 6553600 | bytes 2883584 | tf_op jit(solution)/shard_map/pallas_call | solution.py:384
  14.0 0.9 %copy.7 = f32[3,16,32,128]{3,2,1,0:T(8,128)} copy(f32[3,16,32,128]{3,2,1,0:T(8,128)S(1)} %shard_map.55) | data formatting | bytes 1572864

commit v8 on v7

--- a/solution.py
+++ b/solution.py
@@ -7,7 +7,7 @@
 from jax.sharding import PartitionSpec as P
 
 MESH = pl.DeviceIdType.MESH
-GROUP = 4
+GROUP = 8
 EDGE = 8
 UNROLL = 16
 

time: 15.1 us -> 15.6 us (1.033)
  the two profiles are of different devices: /device:TPU:8 before, /device:TPU:16 now
where the time goes in v8:
time: 15.6 us; the launch traced here: 15.4 us
  Pallas kernels  14.5 us (93%)
  local copies, waits for them, and re-layouts  0.88 us (6%)
    pallas_call x1, Pallas kernels, per_device(): pl.pallas_call(functools.partial(kernel, groups, group, lats), out_shape=...  14.5 us
    unnamed x1, local copies, waits for them, and re-layouts  0.88 us

profile of v8, /device:TPU:16, one launch (start us, length us, event | category | flops | bytes accessed | tf_op | source)
XLA Modules:
  0.0 15.4 jit_solution(4363871543217442318)
XLA Ops:
  0.0 14.5 %shard_map.55 = f32[3,16,32,128]{3,2,1,0:T(8,128)S(1)} custom-call(f32[3,16,32,128]{3,2,1,0:T(8,128)} %conc.1, f32[3,16,32,128]{3,2,1,0:T(8,128)} %courant.1, f32[2,16,32,128]{3,2,1,0:T(8,128)} %rates.1, f32[32,128]{1,0:T(8,128)} %spread.1, f32[3,32,128]{2,1,0:T(8,128)} %inlet.1), custom_call_target="tpu_custom_call" | custom-call | flops 6553600 | bytes 2883584 | tf_op jit(solution)/shard_map/pallas_call | solution.py:384
  14.6 0.9 %copy.7 = f32[3,16,32,128]{3,2,1,0:T(8,128)} copy(f32[3,16,32,128]{3,2,1,0:T(8,128)S(1)} %shard_map.55) | data formatting | bytes 1572864

commit v9 on v7

--- a/solution.py
+++ b/solution.py
@@ -80,9 +80,12 @@
     for step in range(1, group):
         peer = outer * group + lax.rem(inner + step, group)
         pl.semaphore_signal(barrier, inc=1, device_id={"flow": peer}, device_id_type=MESH)
-    for step in range(1, groups):
-        peer = lax.rem(outer + step, groups) * group + inner
-        pl.semaphore_signal(barrier, inc=1, device_id={"flow": peer}, device_id_type=MESH)
+    for o in range(groups - 1):
+        @pl.when(o < outer)
+        def _():
+            pl.semaphore_signal(
+                barrier, inc=1, device_id={"flow": o * group + inner}, device_id_type=MESH
+            )
 
     @pl.when(not_low)
     def _():
@@ -109,7 +112,7 @@
         pad[:, :, EDGE + rows:2 * EDGE + rows] = nothing
 
     beside = jnp.where(not_low, 1, 0) + jnp.where(not_high, 1, 0)
-    pl.semaphore_wait(barrier, group - 1 + groups - 1 + beside)
+    pl.semaphore_wait(barrier, group - 1 + groups - 1 - outer + beside)
 
     to_high = pltpu.make_async_remote_copy(
         src_ref=conc.at[:, :, rows - 1:rows], dst_ref=pad.at[:, :, EDGE - 1:EDGE],

time: 15.1 us -> 15.1 us (level)
  no operation moved by 1% of the time
where the time goes in v9:
time: 15.1 us; the launch traced here: 14.8 us
  Pallas kernels  14 us (93%)
  local copies, waits for them, and re-layouts  0.88 us (6%)
    pallas_call x1, Pallas kernels, per_device(): pl.pallas_call(functools.partial(kernel, groups, group, lats), out_shape=...  14 us
    unnamed x1, local copies, waits for them, and re-layouts  0.88 us

profile of v9, /device:TPU:8, one launch (start us, length us, event | category | flops | bytes accessed | tf_op | source)
XLA Modules:
  0.0 14.8 jit_solution(8319777201014199398)
XLA Ops:
  0.0 14.0 %shard_map.55 = f32[3,16,32,128]{3,2,1,0:T(8,128)S(1)} custom-call(f32[3,16,32,128]{3,2,1,0:T(8,128)} %conc.1, f32[3,16,32,128]{3,2,1,0:T(8,128)} %courant.1, f32[2,16,32,128]{3,2,1,0:T(8,128)} %rates.1, f32[32,128]{1,0:T(8,128)} %spread.1, f32[3,32,128]{2,1,0:T(8,128)} %inlet.1), custom_call_target="tpu_custom_call" | custom-call | flops 6553600 | bytes 2883584 | tf_op jit(solution)/shard_map/pallas_call | solution.py:387
  14.0 0.9 %copy.7 = f32[3,16,32,128]{3,2,1,0:T(8,128)} copy(f32[3,16,32,128]{3,2,1,0:T(8,128)S(1)} %shard_map.55) | data formatting | bytes 1572864
